TPU v7x, 32 devices: a whole 2x2x4 slice. The times are simulated.
32 devices in a mesh: state: 2 (over y), mode: 16 (over z, x, core).
Axes of the slice: x: 2, y: 2, z: 4, core: 2. Of those that a mesh axis runs over, the one named last changes fastest.
Arguments:
- coeffs: float32 [2, 128, 4096], P('state', 'mode'), may hold values from -0.375 to 0.375
- diag_h2: float32 [2, 32, 4096], P('state'), may hold values from -0.75 to 0.75
- diag_h3: float32 [2, 32, 4096], P('state'), may hold values from -0.75 to 0.75
- diag_v1: float32 [2, 32, 128], P('state', None, 'mode'), may hold values from -1.5 to 1.5
- coup_h2: float32 [32, 4096], replicated, may hold values from -0.75 to 0.75
- coup_h3: float32 [32, 4096], replicated, may hold values from -0.75 to 0.75
- coup_v1: float32 [32, 128], P(None, 'mode'), may hold values from -1.5 to 1.5
- pairs: int32 [32, 3], replicated, may hold values from 0 to 31, as said below
Outputs:
- action: float32 [2, 128, 4096], P('state', 'mode')
- diag_field: float32 [2, 64, 2048], P('state', 'mode')
- pair_field: float32 [2, 64, 1984], P('state', 'mode')
Inputs may be any that keep to these rules, and one draw needn't show every extreme that they name: `pairs`: each row is (target state, source state, coupling term); the source differs from the target; every state is the target of at most 31 rows, and one state of exactly 31.
All inputs are finite; a program needn't handle non-finite values.
Results may differ from a plain program's by a relative error of at most 0.0001.
Values sent between devices are 32-bit elements; how exact they have to be, the bound alone decides.
A program may use at most 64 MiB of HBM per device.

v0:
```python
import jax
import jax.numpy as jnp
from jax import lax
from jax.sharding import PartitionSpec as P

N2 = 64
N3 = 64
PAIRS_MEAN = 16


HIGH = lax.Precision.HIGH


def reduce_rows(partials):
    both = jnp.concatenate(partials, axis=1)
    rows = lax.psum_scatter(both, "mode", scatter_dimension=0, tiled=True)
    return rows[:, : partials[0].shape[1]], rows[:, partials[0].shape[1] :]


def pair_block(gathered, coup_h2, coup_h3, coup_v1, chosen, is_valid):
    target_ids = chosen[:, 0]
    source_ids = chosen[:, 1]
    term_ids = chosen[:, 2]
    product = jnp.einsum("pgac,pdc->pgad", gathered[source_ids], coup_h3[term_ids], precision=HIGH)
    weights = coup_v1[term_ids] * is_valid[:, None]
    action = (
        jnp.einsum("pea,pgad->pged", coup_h2[term_ids], product, precision=HIGH)
        * weights[:, :, None, None]
    )
    weighted = gathered[target_ids] * weights[:, :, None, None]
    fields = jnp.einsum("pgac,pgbc->pab", weighted, product, precision=HIGH)
    return (action, fields)


def per_device(coeffs, diag_h2, diag_h3, diag_v1, coup_h2, coup_h3, coup_v1, pairs):
    rows_here = coeffs.shape[1]
    width2 = N2
    width3 = N3
    own_terms = diag_h2.shape[1]
    left_ops = diag_h2[0].reshape(own_terms, width2, width2)
    right_ops = diag_h3[0].reshape(own_terms, width3, width3)
    coup_left = coup_h2.reshape(coup_h2.shape[0], width2, width2)
    coup_right = coup_h3.reshape(coup_h3.shape[0], width3, width3)
    states = lax.axis_size("state")
    npairs = pairs.shape[0]
    most_slots = min(3 * PAIRS_MEAN, states * PAIRS_MEAN - 1)
    myself = lax.axis_index("state")
    tensor = coeffs[0].reshape(rows_here, width2, width3)
    gathered = lax.all_gather(coeffs, "state", axis=0, tiled=True).reshape(
        states, rows_here, width2, width3
    )
    diag_product = jnp.einsum("gac,tdc->tgad", tensor, right_ops, precision=HIGH)
    diag_terms = jnp.einsum("tea,tgad->tged", left_ops, diag_product, precision=HIGH)
    diag_action = jnp.sum(diag_terms * diag_v1[0][:, :, None, None], axis=0)
    diag_weighted = tensor[None] * diag_v1[0][:, :, None, None]
    diag_fields = jnp.einsum("tgac,tgbc->atb", diag_weighted, diag_product, precision=HIGH)
    diag_fields = diag_fields.reshape(width2, own_terms * width2)
    is_mine = pairs[:, 0] == myself
    slot_rank = jnp.cumsum(is_mine.astype(jnp.int32)) - 1
    owned_ids = jnp.arange(PAIRS_MEAN, dtype=jnp.int32) * states + myself
    chosen = pairs[owned_ids]
    is_valid = jnp.ones((PAIRS_MEAN,), jnp.float32)
    state_ids = jnp.arange(states, dtype=jnp.int32)

    def run_block(block_index, carried):
        pair_sum, fields = carried
        first_slot = block_index * 8
        part_chosen = lax.dynamic_slice_in_dim(chosen, first_slot, 8, 0)
        part_valid = lax.dynamic_slice_in_dim(is_valid, first_slot, 8, 0)
        action, block_fields = pair_block(
            gathered, coup_left, coup_right, coup_v1, part_chosen, part_valid
        )
        onehot = (part_chosen[:, 0][:, None] == state_ids[None, :]).astype(jnp.float32)
        pair_sum = pair_sum + jnp.einsum("ps,pged->sged", onehot, action, precision=HIGH)
        fields = lax.dynamic_update_slice_in_dim(fields, block_fields, first_slot, 0)
        return (pair_sum, fields)

    start_sum = jnp.zeros((states, rows_here, width2, width3), jnp.float32)
    start_fields = jnp.zeros((PAIRS_MEAN, width2, width2), jnp.float32)
    pair_sum, fields = lax.fori_loop(0, PAIRS_MEAN // 8, run_block, (start_sum, start_fields))
    received = lax.psum_scatter(
        pair_sum.reshape(states, rows_here, width2 * width3),
        "state",
        scatter_dimension=0,
        tiled=True,
    )
    accumulated = diag_action + received[0].reshape(rows_here, width2, width3)
    spread_fields = fields.transpose(1, 0, 2).reshape(width2, PAIRS_MEAN * width2)
    diag_rows, spread_rows = reduce_rows((diag_fields, spread_fields))
    share_rows = spread_rows.shape[0]
    collected = lax.all_gather(spread_rows[None], "state", axis=0, tiled=True)
    stacked = collected.reshape(states, share_rows, PAIRS_MEAN, width2).transpose(2, 0, 1, 3)
    stacked = stacked.reshape(npairs, share_rows * width2)
    picked_mask = (
        (slot_rank[None, :] == jnp.arange(most_slots, dtype=jnp.int32)[:, None]) & is_mine[None, :]
    ).astype(jnp.float32)
    picked = jnp.dot(picked_mask, stacked, precision=lax.Precision.HIGHEST)
    pair_rows = picked.reshape(most_slots, share_rows, width2).transpose(1, 0, 2)
    pair_rows = pair_rows.reshape(share_rows, most_slots * width2)
    action_out = accumulated.reshape(1, rows_here, width2 * width3)
    return (action_out, diag_rows[None], pair_rows[None])


def solution(mesh):
    placed = (
        P("state", "mode", None),
        P("state", None, None),
        P("state", None, None),
        P("state", None, "mode"),
        P(),
        P(),
        P(None, "mode"),
        P(),
    )
    return jax.shard_map(
        per_device,
        mesh=mesh,
        in_specs=placed,
        out_specs=(P("state", "mode", None), P("state", "mode", None), P("state", "mode", None)),
        check_vma=False,
    )
```

profile of v0, /device:TPU:0, one launch (start us, length us, event | category | flops | bytes accessed | tf_op | source)
XLA Modules:
  0.0 190.0 jit_solution(10095518889353406524)
XLA Ops:
  8.1 1.8 reshape.165
  9.8 7.4 %all_gather.6 = f32[2,8,4096]{2,1,0:T(8,128)S(1)} all-gather(f32[1,8,4096]{2,1,0:T(8,128)} %param.10), channel_id=1, replica_groups=mesh['state'=2,'mode'=16] {'state'}, dimensions={0}, use_global_device_ids=true | all-gather | bytes 393216 | tf_op jit(solution)/shard_map/all_gather | solution.py:49
  21.5 1.4 reshape.164
  26.6 38.0 %while.16 = (s32[]{:T(128)}, f32[2,8,64,64]{3,0,2,1:T(2,128)}, f32[16,64,64]{2,1,0:T(8,128)}, s32[16,3]{0,1:T(4,128)S(1)}, f32[2,8,64,64]{3,2,1,0:T(8,128)S(1)},...) while((s32[]{:T(128)}, f32[2,8,64,64]{3,0,2,1:T(2,128)}, ...), condition=%wide.region_2.3_spmd.clone, body=%wide.region_1.0_spmd.clone.sunk | while | flops 305794144 | bytes 21513964 | solution.py:80
  27.2 1.8 gather_fusion.3
  29.0 1.8 gather_fusion.1
  31.5 2.0 %gather_fusion = f32[8,8,64,64]{3,2,1,0:T(8,128)} fusion(f32[2,8,64,64]{3,2,1,0:T(8,128)S(1)} %get-tuple-element.334, s32[1024]{0:T(1024)S(1)} %pad_clamp_fusion.6), kind=kCustom, calls=%fused_computation.clone.clone.1 | custom fusion | bytes 2097184 | tf_op jit(solution)/shard_map/while/body/eval_jaxpr/gather | solution.py:24
  33.6 2.7 %fusion.65 = f32[8,8,64,64]{3,2,1,0:T(8,128)S(1)} fusion(f32[8,8,64,64]{3,2,1,0:T(8,128)} %gather_fusion, f32[8,64,64]{2,1,0:T(8,128)S(1)} %gather_fusion.1), kind=kOutput, calls=%fused_computation.15.clone.1 | convolution fusion | flops 100663296 | bytes 2228224 | tf_op jit(solution)/shard_map/while/body/eval_jaxpr/pgac,pdc->pgad/dot_general | solution.py:24
  38.2 3.3 %multiply_bitcast_fusion.2 = f32[8,8,64,64]{2,3,1,0:T(8,128)} fusion(f32[8,8,64,64]{3,2,1,0:T(8,128)S(1)} %fusion.65, f32[8,8]{1,0:T(8,128)S(1)} %gather_fusion.2, f32[8,64,64]{2,1,0:T(8,128)S(1)} %gather_fusion.3), kind=kOutput, calls=%fused_computation.9.clone.1 | convolution fusion | flops 100925440 | bytes 2228480 | tf_op jit(solution)/shard_map/while/body/eval_jaxpr/pea,pgad->pged/dot_general | solution.py:27
  41.6 2.1 %copy.74 = f32[8,8,64,64]{3,0,2,1:T(8,128)S(1)} copy(f32[8,8,64,64]{2,3,1,0:T(8,128)} %multiply_bitcast_fusion.2) | data formatting | bytes 2097152 | tf_op jit(solution)/shard_map/while/body/eval_jaxpr/mul | solution.py:27
  46.2 1.8 gather_fusion.3
  48.0 1.8 gather_fusion.1
  50.5 2.0 %gather_fusion = f32[8,8,64,64]{3,2,1,0:T(8,128)} fusion(f32[2,8,64,64]{3,2,1,0:T(8,128)S(1)} %get-tuple-element.334, s32[1024]{0:T(1024)S(1)} %pad_clamp_fusion.6), kind=kCustom, calls=%fused_computation.clone.clone.1 | custom fusion | bytes 2097184 | tf_op jit(solution)/shard_map/while/body/eval_jaxpr/gather | solution.py:24
  52.6 2.7 %fusion.65 = f32[8,8,64,64]{3,2,1,0:T(8,128)S(1)} fusion(f32[8,8,64,64]{3,2,1,0:T(8,128)} %gather_fusion, f32[8,64,64]{2,1,0:T(8,128)S(1)} %gather_fusion.1), kind=kOutput, calls=%fused_computation.15.clone.1 | convolution fusion | flops 100663296 | bytes 2228224 | tf_op jit(solution)/shard_map/while/body/eval_jaxpr/pgac,pdc->pgad/dot_general | solution.py:24
  57.2 3.3 %multiply_bitcast_fusion.2 = f32[8,8,64,64]{2,3,1,0:T(8,128)} fusion(f32[8,8,64,64]{3,2,1,0:T(8,128)S(1)} %fusion.65, f32[8,8]{1,0:T(8,128)S(1)} %gather_fusion.2, f32[8,64,64]{2,1,0:T(8,128)S(1)} %gather_fusion.3), kind=kOutput, calls=%fused_computation.9.clone.1 | convolution fusion | flops 100925440 | bytes 2228480 | tf_op jit(solution)/shard_map/while/body/eval_jaxpr/pea,pgad->pged/dot_general | solution.py:27
  60.6 2.1 %copy.74 = f32[8,8,64,64]{3,0,2,1:T(8,128)S(1)} copy(f32[8,8,64,64]{2,3,1,0:T(8,128)} %multiply_bitcast_fusion.2) | data formatting | bytes 2097152 | tf_op jit(solution)/shard_map/while/body/eval_jaxpr/mul | solution.py:27
  64.6 1.4 copy.55
  66.2 4.5 %fusion.31 = f32[32,64,8,64]{3,1,2,0:T(8,128)S(1)} fusion(f32[8,64,64,1]{2,1,0,3:T(8,128)} %reshape.165, f32[32,64,64,1]{2,1,0,3:T(8,128)S(1)} %copy-done.4), kind=kOutput, calls=%fused_computation.42 | convolution fusion | flops 402653184 | bytes 4849664 | tf_op jit(solution)/shard_map/gac,tdc->tgad/dot_general | solution.py:52
  70.7 7.2 %fusion.21 = f32[32,64,64,1]{2,1,3,0:T(8,128)S(1)} fusion(f32[32,64,8,64]{3,1,2,0:T(8,128)S(1)} %fusion.31, f32[8,64,64]{2,1,0:T(8,128)S(1)} %reshape_squeeze.11, f32[32,8]{1,0:T(8,128)S(1)} %copy.48), kind=kOutput, calls=%fused_computation.32 | convolution fusion | flops 403701760 | bytes 4850688 | tf_op jit(solution)/shard_map/tgac,tgbc->atb/dot_general | solution.py:56
  81.9 6.2 %multiply_reduce_fusion = f32[8,64,64]{2,1,0:T(8,128)S(1)} fusion(f32[32,8]{1,0:T(8,128)S(1)} %copy.48, f32[32,64,8,64]{3,1,2,0:T(8,128)} %copy-done, f32[32,64,64,1]{2,1,0,3:T(8,128)S(1)} %reshape.166), kind=kOutput, calls=%fused_computation.37 | convolution fusion | flops 404717568 | bytes 4850688 | tf_op jit(solution)/shard_map/tea,tgad->tged/dot_general | solution.py:53
  89.6 83.4 %all-reduce.3.cloned.1.call-done = f32[64,3072]{1,0:T(8,128)} async-done(((f32[64,3072]{1,0:T(8,128)}), f32[64,3072]{1,0:T(8,128)}) %all-reduce.3.cloned.1.call-update) | async-done | bytes 786448
  173.9 4.4 %all-gather.1 = f32[2,4,1024]{2,1,0:T(4,128)S(1)} all-gather(f32[1,4,1024]{2,1,0:T(4,128)S(1)} %dynamic-slice_bitcast_fusion.1), channel_id=2, replica_groups=mesh['state'=2,'mode'=16] {'state'}, dimensions={0}, use_global_device_ids=true | all-gather | bytes 49152 | tf_op jit(solution)/shard_map/all_gather | solution.py:91
  179.5 1.5 dynamic-slice_bitcast_fusion
  181.0 1.6 add.97
  (86 shorter events, 25.3 us)
Async XLA Ops:
  8.0 13.5 %copy-start.7 = (f32[1,32,4096]{2,1,0:T(8,128)S(1)}, f32[1,32,4096]{2,1,0:T(8,128)}, u32[]{:S(2)}) copy-start(f32[1,32,4096]{2,1,0:T(8,128)} %param.12) | copy-start | bytes 1572868
  8.0 14.9 %copy-start.8 = (f32[32,4096]{1,0:T(8,128)S(1)}, f32[32,4096]{1,0:T(8,128)}, u32[]{:S(2)}) copy-start(f32[32,4096]{1,0:T(8,128)} %param.14) | copy-start | bytes 1572868
  8.0 165.0 %all-reduce.3.cloned.1.call-start = ((), (), s32[]{:S(2)}) async-start(), calls=%async_computation.2 | async-start | bytes 1572864
  18.2 6.1 %copy-start.9 = (f32[32,4096]{1,0:T(8,128)S(1)}, f32[32,4096]{1,0:T(8,128)}, u32[]{:S(2)}) copy-start(f32[32,4096]{1,0:T(8,128)} %param.15) | copy-start | bytes 1572868
  33.6 2.7 %copy-start.5 = (f32[16,64,64]{2,1,0:T(8,128)S(1)}, f32[16,64,64]{2,1,0:T(8,128)}, u32[]{:S(2)}) copy-start(f32[16,64,64]{2,1,0:T(8,128)} %get-tuple-element.320) | copy-start | bytes 786436 | tf_op jit(solution)/shard_map/while
  37.4 0.8 copy-start.6
  41.6 2.1 %copy-start.1 = (f32[2,8,64,64]{3,0,2,1:T(2,128)S(1)}, f32[2,8,64,64]{3,0,2,1:T(2,128)}, u32[]{:S(2)}) copy-start(f32[2,8,64,64]{3,0,2,1:T(2,128)} %get-tuple-element.319) | copy-start | bytes 786436 | tf_op jit(solution)/shard_map/while
  44.8 0.8 copy-start.2
  52.6 2.7 %copy-start.5 = (f32[16,64,64]{2,1,0:T(8,128)S(1)}, f32[16,64,64]{2,1,0:T(8,128)}, u32[]{:S(2)}) copy-start(f32[16,64,64]{2,1,0:T(8,128)} %get-tuple-element.320) | copy-start | bytes 786436 | tf_op jit(solution)/shard_map/while
  56.4 0.8 copy-start.6
  60.6 2.1 %copy-start.1 = (f32[2,8,64,64]{3,0,2,1:T(2,128)S(1)}, f32[2,8,64,64]{3,0,2,1:T(2,128)}, u32[]{:S(2)}) copy-start(f32[2,8,64,64]{3,0,2,1:T(2,128)} %get-tuple-element.319) | copy-start | bytes 786436 | tf_op jit(solution)/shard_map/while
  63.8 0.8 copy-start.2
  64.6 1.6 copy-start.4
  70.7 7.2 %copy-start = (f32[32,64,8,64]{3,1,2,0:T(8,128)}, f32[32,64,8,64]{3,1,2,0:T(8,128)S(1)}, u32[]{:S(2)}) copy-start(f32[32,64,8,64]{3,1,2,0:T(8,128)S(1)} %fusion.31) | copy-start | bytes 12582916
  78.0 1.6 copy-start.3
  78.3 3.2 %copy-start.10 = (f32[1,32,4096]{2,1,0:T(8,128)S(1)}, f32[1,32,4096]{2,1,0:T(8,128)}, u32[]{:S(2)}) copy-start(f32[1,32,4096]{2,1,0:T(8,128)} %param.11) | copy-start | bytes 1572868
  79.3 101.7 %reduce-scatter.2.cloned.1.call-start = ((), (), s32[]{:S(2)}) async-start(), calls=%async_computation.1 | async-start | bytes 393216 | tf_op jit(solution)/shard_map/reduce_scatter | solution.py:81
  81.9 6.5 %copy-start.11 = (u32[32]{0:T(128)S(1)}, u32[32]{0:T(128)}, u32[]{:S(2)}) copy-start(u32[32]{0:T(128)} %constant.71) | copy-start | bytes 388
Sparse Core Ops, SparseCore 0:
  79.4 93.6 all-reduce.2
Sparse Core Ops, SparseCore 1:
  82.0 13.0 reduce-scatter.1
where the time goes:
time: 191 us; the launch traced here: 190 us
  waiting for transfers between devices  83.5 us (44%)
  local copies, waits for them, and re-layouts  39.8 us (21%)
  matrix products  34.7 us (18%)
  between operations  16.4 us (9%)
  blocking collectives  11.8 us (6%)
  other arithmetic  3.41 us (2%)
    unnamed x3, waiting for transfers between devices  83.5 us
    all_gather x1, blocking collectives, per_device(): lax.all_gather(coeffs, 'state', axis=0, tiled=True)  7.38 us
    dot_general x1, matrix products, per_device(): jnp.einsum('tgac,tgbc->atb', diag_weighted, diag_product, precision=HIGH)  7.23 us
    dot_general x2, matrix products, pair_block(): jnp.einsum('pea,pgad->pged', coup_h2[term_ids], product, precision=HIGH)  6.69 us
    dot_general x1, matrix products, per_device(): jnp.einsum('tea,tgad->tged', left_ops, diag_product, precision=HIGH)  6.18 us
    dot_general x2, matrix products, pair_block(): jnp.einsum('pgac,pdc->pgad', gathered[source_ids], coup_h3[term_ids], pre...  5.31 us
    dot_general x1, matrix products, per_device(): jnp.einsum('gac,tdc->tgad', tensor, right_ops, precision=HIGH)  4.49 us
    all_gather x1, blocking collectives, per_device(): collected = lax.all_gather(spread_rows[None], 'state', axis=0, tiled=True)  4.41 us
  transfers between devices with their start and end apart: 2, of which 1 were waited for; matrix products, arithmetic and copies ran while one was open for 7% of the time, Pallas kernels for 0%

commit v1 on v0

v1 whole, which is shorter than its diff:
```python
import functools

import jax
import jax.numpy as jnp
from jax import lax
from jax.experimental import pallas as pl
from jax.experimental.pallas import tpu as pltpu
from jax.sharding import PartitionSpec as P

MESH = pl.DeviceIdType.MESH
F32 = jnp.float32
BF16 = jnp.bfloat16


def split(value):
    high = value.astype(BF16)
    return high, (value - high.astype(F32)).astype(BF16)


def dot_rows(left, right):
    return lax.dot_general(left, right, (((1,), (1,)), ((), ())), preferred_element_type=F32)


def dot(left, right):
    return jnp.dot(left, right, preferred_element_type=F32)


def flag(condition):
    return jnp.where(condition, 1.0, 0.0).astype(F32)


def kernel(
    a_ref, dh2, dh3, ch2, ch3, dv1, cv1, pairs, slots,
    action_ref, diag_ref, pair_ref,
    gath, a3, aa, hh, hp, xh, xl, yh, yl, psum, arecv, gfield, rows3,
    buf0, buf1, buf2, ra0, ra1, ra2, sb0, sb1, sb2, rb0, rb1, rb2, sc0, sc1, sc2, rc0, rc1, rc2,
    send, recv, *, modes
):
    states, grid = gath.shape[0], gath.shape[1]
    n = a_ref.shape[-1]
    half = n // 2
    count = dh2.shape[0] // 2
    pcount = yh.shape[0] // n
    ring = modes // 4
    share = n // modes
    bufs, ras, sbs = (buf0, buf1, buf2), (ra0, ra1, ra2), (sb0, sb1, sb2)
    rbs, scs, rcs = (rb0, rb1, rb2), (sc0, sc1, sc2), (rc0, rc1, rc2)

    st = lax.axis_index("state")
    md = lax.axis_index("mode")
    core = lax.rem(md, 2)
    x = lax.rem(lax.div(md, 2), 2)
    z = lax.div(md, 4)
    sibling = (st, md + 1 - 2 * core)
    across = (st, md + 2 - 4 * x)
    others = [(lax.rem(st + d, states), md) for d in range(1, states)]
    along = [(st, lax.rem(z + d, ring) * 4 + x * 2 + core) for d in range(1, ring)]
    partners = others + [sibling, across] + along

    barrier = pltpu.get_barrier_semaphore()
    for device in partners:
        pl.semaphore_signal(barrier, inc=1, device_id=device, device_id_type=MESH)

    numbers = iter(range(10000))

    def copy_to(device, source, target):
        at = next(numbers)
        return pltpu.make_async_remote_copy(
            src_ref=source, dst_ref=target, send_sem=send.at[at], recv_sem=recv.at[at],
            device_id=device, device_id_type=MESH,
        )

    def pack(value):
        return jnp.concatenate([value[:half], value[half:]], axis=1)

    lane = lax.broadcasted_iota(jnp.int32, (1, 2 * n), 1)

    def lanes(first, second):
        return jnp.where(lane < n, first, second)

    def load_state(s, g, value):
        high, low = split(value)
        rows = pl.ds(g * n, n)
        a3[s, rows, 0:n] = high
        a3[s, rows, n : 2 * n] = low
        a3[s, rows, 2 * n : 3 * n] = high
        for t in range(2):
            aa[s, t * n : (t + 1) * n, g * 2 * n + t * n : g * 2 * n + (t + 1) * n] = high
            aa[s, (2 + t) * n : (3 + t) * n, g * 2 * n + t * n : g * 2 * n + (t + 1) * n] = low

    def weights_three(value):
        high, low = split(value)
        return jnp.concatenate([high, high, low], axis=1)

    def store_x(high_ref, low_ref, product, q, weight):
        for k in range(2):
            rows = pl.ds(pl.multiple_of((2 * q + k) * n, n), n)
            for g in range(grid):
                block = product[g * n : (g + 1) * n, k * 2 * n : (k + 1) * 2 * n]
                block = block * lanes(weight(k, 0, g), weight(k, 1, g))
                high, low = split(block)
                high_ref[rows, g * 2 * n : (g + 1) * 2 * n] = high
                low_ref[rows, g * 2 * n : (g + 1) * 2 * n] = low

    def field(high_ref, low_ref, s, i):
        rows = pl.ds(pl.multiple_of(i * 2 * n, 2 * n), 2 * n)
        both = dot_rows(high_ref[rows, :], aa[s])
        return both[:, : 2 * n] + both[:, 2 * n :] + dot_rows(low_ref[rows, :], aa[s, 0 : 2 * n])

    def store_field(targets, block, i):
        turned = block.T
        for t in range(2):
            ref, start = targets[t]
            columns = pl.ds(pl.multiple_of(start + i * 2 * n, 2 * n), 2 * n)
            for m in range(modes):
                top = t * n + m * share
                ref[m % 2, m // 2 % 2, m // 4, :, columns] = turned[top : top + share]

    def act(left, high_ref, low_ref, gp):
        columns = pl.ds(pl.multiple_of(gp * 4 * n, 4 * n), 4 * n)
        both = dot(left[...], high_ref[:, columns])
        total = both[: 2 * n] + both[2 * n :] + dot(left[0 : 2 * n], low_ref[:, columns])
        return [
            total[0:n, k * 2 * n : k * 2 * n + n] + total[n : 2 * n, k * 2 * n + n : (k + 1) * 2 * n]
            for k in range(2)
        ]

    for g in range(grid):
        gath[st, g] = pack(a_ref[g])
    pl.semaphore_wait(barrier, len(partners))
    coeff_copies = [copy_to(device, gath.at[st], gath.at[st]) for device in others]
    for c in coeff_copies:
        c.start()

    aa[...] = jnp.zeros_like(aa)
    for g in range(grid):
        load_state(st, g, a_ref[g])

    def diag_group(q, carry):
        value = jnp.concatenate(
            [dh3[t * count + 2 * q + k] for k in range(2) for t in range(2)], axis=0
        )
        product = dot_rows(a3[st], weights_three(value))
        store_x(xh, xl, product, q, lambda k, t, g: dv1[t * count + 2 * q + k, g])
        return carry

    lax.fori_loop(0, count // 2, diag_group, 0)

    def diag_field(i, carry):
        store_field(((buf0, 0), (buf1, 0)), field(xh, xl, st, i), i)
        return carry

    lax.fori_loop(0, count // 2, diag_field, 0)

    def core_start(i):
        c = copy_to(sibling, bufs[i].at[1 - core], ras[i])
        c.start()
        return c

    def x_start(i, c):
        c.wait()
        sbs[i][...] = bufs[i][core] + ras[i][...]
        c = copy_to(across, sbs[i].at[1 - x], rbs[i])
        c.start()
        return c

    def z_start(i, c):
        c.wait()
        scs[i][...] = sbs[i][x] + rbs[i][...]
        copies = [
            copy_to(device, scs[i].at[lax.rem(z + d + 1, ring)], rcs[i].at[d])
            for d, device in enumerate(along)
        ]
        for c in copies:
            c.start()
        return copies

    def finish(i, copies):
        for c in copies:
            c.wait()
        total = scs[i][z]
        for d in range(ring - 1):
            total = total + rcs[i][d]
        return total

    flight = [core_start(0), core_start(1)]

    for t in range(2):
        for j in range(count):
            high, low = split(dh2[t * count + j])
            hh[t * n : (t + 1) * n, j * n : (j + 1) * n] = high
            hh[(2 + t) * n : (3 + t) * n, j * n : (j + 1) * n] = low
    flight = [x_start(i, flight[i]) for i in range(2)]

    def diag_act(gp, carry):
        first, second = act(hh, xh, xl, gp)
        action_ref[2 * gp] = first
        action_ref[2 * gp + 1] = second
        return carry

    lax.fori_loop(0, grid // 2, diag_act, 0)

    for c in coeff_copies:
        c.wait()
    for d in range(1, states):
        s = lax.rem(st + d, states)
        for g in range(grid):
            packed = gath[s, g]
            load_state(s, g, jnp.concatenate([packed[:, :n], packed[:, n:]], axis=0))

    def row_of(q, k, t):
        return (t * pcount + 2 * q + k) * states + st

    def pair_group(q, carry):
        rows = [row_of(q, k, t) for k in range(2) for t in range(2)]
        value = [ch3[pairs[row, 2]] for row in rows]
        product = None
        for s in range(states):
            masked = jnp.concatenate(
                [v * flag(pairs[row, 1] == s) for v, row in zip(value, rows)], axis=0
            )
            part = dot_rows(a3[s], weights_three(masked))
            product = part if product is None else product + part
        store_x(yh, yl, product, q, lambda k, t, g: cv1[pairs[row_of(q, k, t), 2], g])
        return carry

    lax.fori_loop(0, pcount // 2, pair_group, 0)
    flight = [z_start(i, flight[i]) for i in range(2)]

    def pair_field(i, carry):
        total = None
        for s in range(states):
            mask = [
                lanes(*[flag(pairs[row_of(i, k, t), 0] == s) for t in range(2)]) for k in range(2)
            ]
            block = field(yh, yl, s, i)
            block = jnp.concatenate([block[:n] * mask[0], block[n:] * mask[1]], axis=0)
            total = block if total is None else total + block
        store_field(((buf2, 0), (buf2, pcount * n)), total, i)
        return carry

    lax.fori_loop(0, pcount // 2, pair_field, 0)
    pair_flight = core_start(2)

    for t in range(2):
        for j in range(pcount):
            row = (t * pcount + j) * states + st
            high, low = split(ch2[pairs[row, 2]])
            for s in range(states):
                keep = flag(pairs[row, 0] == s).astype(BF16)
                hp[s, t * n : (t + 1) * n, j * n : (j + 1) * n] = high * keep
                hp[s, (2 + t) * n : (3 + t) * n, j * n : (j + 1) * n] = low * keep
    pair_flight = x_start(2, pair_flight)

    act_copies = []
    for d in list(range(1, states)) + [0]:
        s = lax.rem(st + d, states)

        def pair_act(gp, carry, s=s, d=d):
            for k, block in enumerate(act(hp.at[s], yh, yl, gp)):
                if d == 0:
                    action_ref[2 * gp + k] = action_ref[2 * gp + k] + block
                else:
                    psum[d - 1, 2 * gp + k] = pack(block)
            return carry

        lax.fori_loop(0, grid // 2, pair_act, 0)
        if d > 0:
            c = copy_to(others[d - 1], psum.at[d - 1], arecv.at[d - 1])
            c.start()
            act_copies.append(c)

    pair_flight = z_start(2, pair_flight)
    diag_ref[:, 0 : count * n] = finish(0, flight[0])
    diag_ref[:, count * n : 2 * count * n] = finish(1, flight[1])

    gfield[st] = finish(2, pair_flight)
    field_copies = [copy_to(device, gfield.at[st], gfield.at[st]) for device in others]
    for c in field_copies:
        c.start()
    for c in act_copies:
        c.wait()
    for d in range(states - 1):
        for g in range(grid):
            packed = arecv[d, g]
            action_ref[g] = action_ref[g] + jnp.concatenate([packed[:, :n], packed[:, n:]], axis=0)
    for c in field_copies:
        c.wait()
    for i in range(2 * pcount):
        for s in range(states):
            rows3[i * states + s] = gfield[s, :, i * n : (i + 1) * n]
    for i in range(slots.shape[0]):
        row = slots[i]
        value = rows3[jnp.maximum(row, 0)]
        pair_ref[:, i * n : (i + 1) * n] = jnp.where(row >= 0, value, 0.0)


def per_device(coeffs, diag_h2, diag_h3, diag_v1, coup_h2, coup_h3, coup_v1, pairs, n, modes, states):
    grid = coeffs.shape[1]
    terms = diag_h2.shape[1]
    npairs = pairs.shape[0]
    owned = npairs // states
    most_slots = min(3 * owned, npairs - 1)
    share = n // modes
    ring = modes // 4
    order = jnp.arange(npairs, dtype=jnp.int32)
    mine = pairs[:, 0] == lax.axis_index("state")
    rank = jnp.sum(jnp.where(mine[None, :] & (order[None, :] < order[:, None]), 1, 0), axis=1)
    hit = mine[None, :] & (rank[None, :] == jnp.arange(most_slots, dtype=jnp.int32)[:, None])
    slots = jnp.sum(jnp.where(hit, order[None, :] + 1, 0), axis=1).astype(jnp.int32) - 1

    widths = (terms // 2 * n, terms // 2 * n, owned * n)
    vmem = pltpu.VMEM
    scratch = [
        vmem((states, grid, n // 2, 2 * n), F32),
        vmem((states, grid * n, 3 * n), BF16),
        vmem((states, 4 * n, grid * 2 * n), BF16),
        vmem((4 * n, terms // 2 * n), BF16),
        vmem((states, 4 * n, owned // 2 * n), BF16),
        vmem((terms // 2 * n, grid * 2 * n), BF16),
        vmem((terms // 2 * n, grid * 2 * n), BF16),
        vmem((owned // 2 * n, grid * 2 * n), BF16),
        vmem((owned // 2 * n, grid * 2 * n), BF16),
        vmem((states - 1, grid, n // 2, 2 * n), F32),
        vmem((states - 1, grid, n // 2, 2 * n), F32),
        vmem((states, share, owned * n), F32),
        vmem((npairs, share, n), F32),
    ]
    for lead in ((2, 2, ring), (2, ring), (2, ring), (ring,), (ring,), (ring - 1,)):
        scratch += [vmem(lead + (share, w), F32) for w in widths]
    copies = 3 * (states - 1) + 3 * (ring + 1)
    scratch += [pltpu.SemaphoreType.DMA((copies,)), pltpu.SemaphoreType.DMA((copies,))]
    in_vmem = pl.BlockSpec(memory_space=pltpu.VMEM)
    in_smem = pl.BlockSpec(memory_space=pltpu.SMEM)
    action, diag, pair = pl.pallas_call(
        functools.partial(kernel, modes=modes),
        out_shape=(
            jax.ShapeDtypeStruct((grid, n, n), F32),
            jax.ShapeDtypeStruct((share, terms * n), F32),
            jax.ShapeDtypeStruct((share, most_slots * n), F32),
        ),
        in_specs=[in_vmem] * 5 + [in_smem] * 4,
        out_specs=(in_vmem,) * 3,
        scratch_shapes=scratch,
        compiler_params=pltpu.CompilerParams(
            collective_id=0, has_side_effects=True, vmem_limit_bytes=48 * 1024 * 1024
        ),
    )(
        coeffs.reshape(grid, n, n),
        diag_h2.reshape(terms, n, n),
        diag_h3.reshape(terms, n, n),
        coup_h2.reshape(-1, n, n),
        coup_h3.reshape(-1, n, n),
        diag_v1[0],
        coup_v1,
        pairs,
        slots,
    )
    return action.reshape(1, grid, n * n), diag[None], pair[None]


def solution(mesh):
    placed = (
        P("state", "mode", None),
        P("state", None, None),
        P("state", None, None),
        P("state", None, "mode"),
        P(),
        P(),
        P(None, "mode"),
        P(),
    )
    body = functools.partial(
        per_device, n=64, modes=mesh.shape["mode"], states=mesh.shape["state"]
    )
    return jax.shard_map(
        body,
        mesh=mesh,
        in_specs=placed,
        out_specs=(P("state", "mode", None),) * 3,
        check_vma=False,
    )
```

time: 191 us -> 48.7 us (0.25)
  waiting for transfers between devices: 83.5 us -> 0 us
  matrix products: 34.7 us -> 0 us
  Pallas kernels: 0 us -> 33.7 us
  local copies, waits for them, and re-layouts: 39.8 us -> 13.7 us
  between operations: 16.4 us -> 0.72 us
  blocking collectives: 11.8 us -> 0 us
  other arithmetic: 3.41 us -> 0.24 us
    unnamed x3 -> x0, waiting for transfers between devices: 83.5 us -> none
    dot_general x12 -> x0, matrix products: 34.7 us -> none  [the longest x1 7.23 us: per_device(): jnp.einsum('tgac,tgbc->atb', diag_weighted, diag_product, precision=HIGH)]
    pallas_call x0 -> x1, Pallas kernels: none -> 33.7 us  [per_device(): pl.pallas_call(functools.partial(kernel, modes=modes), out_shape=(jax.Sha...]
    gather x11 -> x0, local copies, waits for them, and re-layouts: 14.3 us -> none  [the longest x2 4.06 us: pair_block(): gathered[source_ids]]
    all_gather x2 -> x0, blocking collectives: 11.8 us -> none  [the longest x1 7.38 us: per_device(): lax.all_gather(coeffs, 'state', axis=0, tiled=True)]
    another operation x5 -> x0, local copies, waits for them, and re-layouts: 5.31 us -> none  [the longest x2 2.78 us: per_device(): tensor = coeffs[0].reshape(rows_here, width2, width3)]
    mul x3 -> x0, local copies, waits for them, and re-layouts: 4.98 us -> none  [the longest x2 4.17 us: pair_block(): jnp.einsum('pea,pgad->pged', coup_h2[term_ids], product, precision=HIGH)]
    reshape x9 -> x6, local copies, waits for them, and re-layouts: 4.61 us -> 8.55 us  [the longest x1 2.45 us: per_device(): coup_h3.reshape(-1, n, n)]
  transfers between devices with their start and end apart: 2 -> 0, of which waited for: 1 -> 0; matrix products, arithmetic and copies ran while one was open for 7% -> 0% of each run, Pallas kernels for 0% -> 0%
where the time goes in v1:
time: 48.7 us; the launch traced here: 48.3 us
  Pallas kernels  33.7 us (69%)
  local copies, waits for them, and re-layouts  13.7 us (28%)
  between operations  0.72 us (1%)
    pallas_call x1, Pallas kernels, per_device(): pl.pallas_call(functools.partial(kernel, modes=modes), out_shape=(jax.Sha...  33.7 us
    unnamed x17, local copies, waits for them, and re-layouts  5.1 us
    reshape x1, local copies, waits for them, and re-layouts, per_device(): coup_h3.reshape(-1, n, n)  2.45 us
    reshape x1, local copies, waits for them, and re-layouts, per_device(): return (action.reshape(1, grid, n * n), diag[None], pair[None])  1.72 us
    reshape x1, local copies, waits for them, and re-layouts, per_device(): diag_h2.reshape(terms, n, n)  1.51 us
    reshape x1, local copies, waits for them, and re-layouts, per_device(): coup_h2.reshape(-1, n, n)  1.46 us
    reshape x1, local copies, waits for them, and re-layouts, per_device(): coeffs.reshape(grid, n, n)  1.01 us

profile of v1, /device:TPU:0, one launch (start us, length us, event | category | flops | bytes accessed | tf_op | source)
XLA Modules:
  0.0 48.3 jit_solution(1375094358107130277)
XLA Ops:
  0.6 0.0 copy-start.5
  0.6 0.7 %copy-done.5 = s32[32,3]{0,1:T(4,128)S(1)} copy-done((s32[32,3]{0,1:T(4,128)S(1)}, s32[32,3]{0,1:T(4,128)}, u32[]{:S(2)}) %copy-start.5) | copy-done | bytes 408
  1.3 0.0 copy-start.3
  1.3 0.1 select_reduce_fusion.1
  1.4 0.1 select_reduce_fusion
  1.6 0.4 copy-done.3
  2.0 0.1 copy.14
  2.1 0.6 %copy-done.4 = f32[32,8]{0,1:T(8,128)S(1)} copy-done((f32[32,8]{0,1:T(8,128)S(1)}, f32[32,8]{0,1:T(8,128)}, u32[]{:S(2)}) %copy-start.4) | copy-done | bytes 1048
  2.7 0.1 copy.15.cv1
  2.8 0.1 copy.16.pairs
  2.9 1.0 %reshape.37.a_ref = f32[8,64,64]{2,1,0:T(8,128)S(1)} reshape(f32[1,8,4096]{2,1,0:T(8,128)} %param.8) | data formatting | bytes 262144 | tf_op jit(solution)/shard_map/reshape | solution.py:349
  3.9 0.0 copy-start.2
  3.9 1.5 %reshape.38.dh2 = f32[32,64,64]{2,1,0:T(8,128)S(1)} reshape(f32[1,32,4096]{2,1,0:T(8,128)} %param.9) | data formatting | bytes 1048576 | tf_op jit(solution)/shard_map/reshape | solution.py:350
  5.4 0.0 copy-done.2
  5.4 0.4 reshape.39.dh3
  5.8 1.5 %reshape.40.ch2 = f32[32,64,64]{2,1,0:T(8,128)S(1)} reshape(f32[32,4096]{1,0:T(8,128)} %param.12) | data formatting | bytes 1048576 | tf_op jit(solution)/shard_map/reshape | solution.py:352
  7.3 2.4 %reshape.41.ch3 = f32[32,64,64]{2,1,0:T(8,128)} reshape(f32[32,4096]{1,0:T(8,128)} %param.13) | data formatting | bytes 1048576 | tf_op jit(solution)/shard_map/reshape | solution.py:353
  9.7 1.2 %copy-done = f32[32,64,64]{2,1,0:T(8,128)S(1)} copy-done((f32[32,64,64]{2,1,0:T(8,128)S(1)}, f32[32,64,64]{2,1,0:T(8,128)}, u32[]{:S(2)}) %copy-start) | copy-done | bytes 524312
  11.0 33.7 %shard_map.103 = (f32[8,64,64]{2,1,0:T(8,128)S(1)}, f32[4,2048]{1,0:T(4,128)S(1)}, f32[4,1984]{1,0:T(4,128)S(1)}) custom-call(f32[8,64,64]{2,1,0:T(8,128)S(1)} %reshape.37.a_ref, f32[32,64,64]{2,1,0:T(8,128)S(1)} %reshape.38.dh2, f32[32,64,64]{2,1,0:T(8,128)S(1)} %reshape.39.dh3, f32[32,64,64]{2,1,0:T(8,128)S(1)} %reshape.40.ch2, f32[32,64,64]{2,1,0:T(8,128)S(1)} %copy-done, ...), custom_call_target="tpu_custom_call" | custom-call | tf_op jit(solution)/shard_map/pallas_call | solution.py:335
  44.7 0.0 copy-start.1
  44.7 0.7 %copy-done.1 = f32[8,64,64]{2,1,0:T(8,128)} copy-done((f32[8,64,64]{2,1,0:T(8,128)}, f32[8,64,64]{2,1,0:T(8,128)S(1)}, u32[]{:S(2)}) %copy-start.1) | copy-done | bytes 131096
  45.4 1.7 %reshape.42 = f32[1,8,4096]{2,1,0:T(8,128)} reshape(f32[8,64,64]{2,1,0:T(8,128)} %copy-done.1) | data formatting | bytes 262144 | tf_op jit(solution)/shard_map/reshape | solution.py:359
  47.1 0.6 %copy.19 = f32[1,4,2048]{2,1,0:T(4,128)} copy(f32[1,4,2048]{2,1,0:T(4,128)S(1)} %bitcast.7) | data formatting | bytes 65536
  47.7 0.6 %copy.20 = f32[1,4,1984]{2,1,0:T(4,128)} copy(f32[1,4,1984]{2,1,0:T(4,128)S(1)} %bitcast.6) | data formatting | bytes 63488
  (5 shorter events, 0.0 us)
Async XLA Ops:
  0.6 0.7 %copy-start.5 = (s32[32,3]{0,1:T(4,128)S(1)}, s32[32,3]{0,1:T(4,128)}, u32[]{:S(2)}) copy-start(s32[32,3]{0,1:T(4,128)} %param.15) | copy-start | bytes 1156
  1.3 0.7 %copy-start.3 = (f32[1,32,8]{1,2,0:T(8,128)S(1)}, f32[1,32,8]{1,2,0:T(8,128)}, u32[]{:S(2)}) copy-start(f32[1,32,8]{1,2,0:T(8,128)} %param.11) | copy-start | bytes 3076
  2.0 0.7 %copy-start.4 = (f32[32,8]{0,1:T(8,128)S(1)}, f32[32,8]{0,1:T(8,128)}, u32[]{:S(2)}) copy-start(f32[32,8]{0,1:T(8,128)} %param.14) | copy-start | bytes 3076
  3.9 1.5 %copy-start.2 = (f32[1,32,4096]{2,1,0:T(8,128)S(1)}, f32[1,32,4096]{2,1,0:T(8,128)}, u32[]{:S(2)}) copy-start(f32[1,32,4096]{2,1,0:T(8,128)} %param.10) | copy-start | bytes 1572868
  9.7 1.2 %copy-start = (f32[32,64,64]{2,1,0:T(8,128)S(1)}, f32[32,64,64]{2,1,0:T(8,128)}, u32[]{:S(2)}) copy-start(f32[32,64,64]{2,1,0:T(8,128)} %reshape.41.ch3) | copy-start | bytes 1572868
  44.7 0.7 %copy-start.1 = (f32[8,64,64]{2,1,0:T(8,128)}, f32[8,64,64]{2,1,0:T(8,128)S(1)}, u32[]{:S(2)}) copy-start(f32[8,64,64]{2,1,0:T(8,128)S(1)} %get-tuple-element.6) | copy-start | bytes 393220

commit v2 on v1

--- a/solution.py
+++ b/solution.py
@@ -32,12 +32,12 @@
 def kernel(
     a_ref, dh2, dh3, ch2, ch3, dv1, cv1, pairs, slots,
     action_ref, diag_ref, pair_ref,
-    gath, a3, aa, hh, hp, xh, xl, yh, yl, psum, arecv, gfield, rows3,
+    gath, d3, c2, c3, acc, a3, aa, hh, hp, xh, xl, yh, yl, psum, arecv, gfield, rows3,
     buf0, buf1, buf2, ra0, ra1, ra2, sb0, sb1, sb2, rb0, rb1, rb2, sc0, sc1, sc2, rc0, rc1, rc2,
     send, recv, *, modes
 ):
     states, grid = gath.shape[0], gath.shape[1]
-    n = a_ref.shape[-1]
+    n = d3.shape[-1]
     half = n // 2
     count = dh2.shape[0] // 2
     pcount = yh.shape[0] // n
@@ -70,6 +70,23 @@
             device_id=device, device_id_type=MESH,
         )
 
+    def loop(total, body, step=4):
+        step = step if total % step == 0 else 1
+
+        def run(i, carry):
+            for k in range(step):
+                body(i * step + k)
+            return carry
+
+        lax.fori_loop(0, total // step, run, 0)
+
+    def matrices(value):
+        return value.reshape(value.shape[0], n, n)
+
+    def spread(source, target):
+        for t in range(0, source.shape[0], 8):
+            target[t : t + 8] = matrices(source[t : t + 8, :])
+
     def pack(value):
         return jnp.concatenate([value[:half], value[half:]], axis=1)
 
@@ -125,32 +142,30 @@
             for k in range(2)
         ]
 
-    for g in range(grid):
-        gath[st, g] = pack(a_ref[g])
+    aa[...] = jnp.zeros_like(aa)
     pl.semaphore_wait(barrier, len(partners))
-    coeff_copies = [copy_to(device, gath.at[st], gath.at[st]) for device in others]
+    coeff_copies = [copy_to(device, a_ref, gath.at[st]) for device in others]
     for c in coeff_copies:
         c.start()
 
-    aa[...] = jnp.zeros_like(aa)
+    tensor = matrices(a_ref[...])
     for g in range(grid):
-        load_state(st, g, a_ref[g])
-
-    def diag_group(q, carry):
+        load_state(st, g, tensor[g])
+    spread(dh3, d3)
+
+    def diag_group(q):
         value = jnp.concatenate(
-            [dh3[t * count + 2 * q + k] for k in range(2) for t in range(2)], axis=0
+            [d3[t * count + 2 * q + k] for k in range(2) for t in range(2)], axis=0
         )
         product = dot_rows(a3[st], weights_three(value))
         store_x(xh, xl, product, q, lambda k, t, g: dv1[t * count + 2 * q + k, g])
-        return carry
-
-    lax.fori_loop(0, count // 2, diag_group, 0)
-
-    def diag_field(i, carry):
+
+    loop(count // 2, diag_group)
+
+    def diag_field(i):
         store_field(((buf0, 0), (buf1, 0)), field(xh, xl, st, i), i)
-        return carry
-
-    lax.fori_loop(0, count // 2, diag_field, 0)
+
+    loop(count // 2, diag_field)
 
     def core_start(i):
         c = copy_to(sibling, bufs[i].at[1 - core], ras[i])
@@ -185,35 +200,24 @@
 
     flight = [core_start(0), core_start(1)]
 
-    for t in range(2):
-        for j in range(count):
-            high, low = split(dh2[t * count + j])
-            hh[t * n : (t + 1) * n, j * n : (j + 1) * n] = high
-            hh[(2 + t) * n : (3 + t) * n, j * n : (j + 1) * n] = low
+    spread(ch3, c3)
+    spread(ch2, c2)
     flight = [x_start(i, flight[i]) for i in range(2)]
-
-    def diag_act(gp, carry):
-        first, second = act(hh, xh, xl, gp)
-        action_ref[2 * gp] = first
-        action_ref[2 * gp + 1] = second
-        return carry
-
-    lax.fori_loop(0, grid // 2, diag_act, 0)
 
     for c in coeff_copies:
         c.wait()
     for d in range(1, states):
         s = lax.rem(st + d, states)
+        tensor = matrices(gath[s])
         for g in range(grid):
-            packed = gath[s, g]
-            load_state(s, g, jnp.concatenate([packed[:, :n], packed[:, n:]], axis=0))
+            load_state(s, g, tensor[g])
 
     def row_of(q, k, t):
         return (t * pcount + 2 * q + k) * states + st
 
-    def pair_group(q, carry):
+    def pair_group(q):
         rows = [row_of(q, k, t) for k in range(2) for t in range(2)]
-        value = [ch3[pairs[row, 2]] for row in rows]
+        value = [c3[pairs[row, 2]] for row in rows]
         product = None
         for s in range(states):
             masked = jnp.concatenate(
@@ -222,12 +226,11 @@
             part = dot_rows(a3[s], weights_three(masked))
             product = part if product is None else product + part
         store_x(yh, yl, product, q, lambda k, t, g: cv1[pairs[row_of(q, k, t), 2], g])
-        return carry
-
-    lax.fori_loop(0, pcount // 2, pair_group, 0)
+
+    loop(pcount // 2, pair_group)
     flight = [z_start(i, flight[i]) for i in range(2)]
 
-    def pair_field(i, carry):
+    def pair_field(i):
         total = None
         for s in range(states):
             mask = [
@@ -237,15 +240,14 @@
             block = jnp.concatenate([block[:n] * mask[0], block[n:] * mask[1]], axis=0)
             total = block if total is None else total + block
         store_field(((buf2, 0), (buf2, pcount * n)), total, i)
-        return carry
-
-    lax.fori_loop(0, pcount // 2, pair_field, 0)
+
+    loop(pcount // 2, pair_field)
     pair_flight = core_start(2)
 
     for t in range(2):
         for j in range(pcount):
             row = (t * pcount + j) * states + st
-            high, low = split(ch2[pairs[row, 2]])
+            high, low = split(c2[pairs[row, 2]])
             for s in range(states):
                 keep = flag(pairs[row, 0] == s).astype(BF16)
                 hp[s, t * n : (t + 1) * n, j * n : (j + 1) * n] = high * keep
@@ -256,34 +258,51 @@
     for d in list(range(1, states)) + [0]:
         s = lax.rem(st + d, states)
 
-        def pair_act(gp, carry, s=s, d=d):
+        def pair_act(gp, s=s, d=d):
             for k, block in enumerate(act(hp.at[s], yh, yl, gp)):
                 if d == 0:
-                    action_ref[2 * gp + k] = action_ref[2 * gp + k] + block
+                    acc[2 * gp + k] = block
                 else:
                     psum[d - 1, 2 * gp + k] = pack(block)
-            return carry
-
-        lax.fori_loop(0, grid // 2, pair_act, 0)
+
+        loop(grid // 2, pair_act)
         if d > 0:
             c = copy_to(others[d - 1], psum.at[d - 1], arecv.at[d - 1])
             c.start()
             act_copies.append(c)
-
-    pair_flight = z_start(2, pair_flight)
-    diag_ref[:, 0 : count * n] = finish(0, flight[0])
-    diag_ref[:, count * n : 2 * count * n] = finish(1, flight[1])
-
+        if d == states - 1:
+            pair_flight = z_start(2, pair_flight)
+
+    for t in range(0, 2 * count, 8):
+        value = matrices(dh2[t : t + 8, :])
+        for k in range(8):
+            top, j = (t + k) // count * n, (t + k) % count
+            high, low = split(value[k])
+            hh[top : top + n, j * n : (j + 1) * n] = high
+            hh[2 * n + top : 3 * n + top, j * n : (j + 1) * n] = low
+
+    def diag_act(gp):
+        for k, block in enumerate(act(hh, xh, xl, gp)):
+            acc[2 * gp + k] = acc[2 * gp + k] + block
+
+    loop(grid // 2, diag_act, 2)
     gfield[st] = finish(2, pair_flight)
     field_copies = [copy_to(device, gfield.at[st], gfield.at[st]) for device in others]
     for c in field_copies:
         c.start()
+    diag_ref[:, 0 : count * n] = finish(0, flight[0])
+    diag_ref[:, count * n : 2 * count * n] = finish(1, flight[1])
     for c in act_copies:
         c.wait()
-    for d in range(states - 1):
-        for g in range(grid):
+    for g in range(grid):
+        total = acc[g]
+        for d in range(states - 1):
             packed = arecv[d, g]
-            action_ref[g] = action_ref[g] + jnp.concatenate([packed[:, :n], packed[:, n:]], axis=0)
+            total = total + jnp.concatenate([packed[:, :n], packed[:, n:]], axis=0)
+        acc[g] = total
+    action_ref[...] = jnp.concatenate(
+        [acc[:, pl.ds(0, half, 2), :], acc[:, pl.ds(1, half, 2), :]], axis=-1
+    ).reshape(grid, n * n)
     for c in field_copies:
         c.wait()
     for i in range(2 * pcount):
@@ -312,7 +331,11 @@
     widths = (terms // 2 * n, terms // 2 * n, owned * n)
     vmem = pltpu.VMEM
     scratch = [
-        vmem((states, grid, n // 2, 2 * n), F32),
+        vmem((states, grid, n * n), F32),
+        vmem((terms, n, n), F32),
+        vmem(coup_h2.shape[:1] + (n, n), F32),
+        vmem(coup_h2.shape[:1] + (n, n), F32),
+        vmem((grid, n, n), F32),
         vmem((states, grid * n, 3 * n), BF16),
         vmem((states, 4 * n, grid * 2 * n), BF16),
         vmem((4 * n, terms // 2 * n), BF16),
@@ -335,7 +358,7 @@
     action, diag, pair = pl.pallas_call(
         functools.partial(kernel, modes=modes),
         out_shape=(
-            jax.ShapeDtypeStruct((grid, n, n), F32),
+            jax.ShapeDtypeStruct((grid, n * n), F32),
             jax.ShapeDtypeStruct((share, terms * n), F32),
             jax.ShapeDtypeStruct((share, most_slots * n), F32),
         ),
@@ -346,17 +369,17 @@
             collective_id=0, has_side_effects=True, vmem_limit_bytes=48 * 1024 * 1024
         ),
     )(
-        coeffs.reshape(grid, n, n),
-        diag_h2.reshape(terms, n, n),
-        diag_h3.reshape(terms, n, n),
-        coup_h2.reshape(-1, n, n),
-        coup_h3.reshape(-1, n, n),
+        coeffs[0],
+        diag_h2[0],
+        diag_h3[0],
+        coup_h2,
+        coup_h3,
         diag_v1[0],
         coup_v1,
         pairs,
         slots,
     )
-    return action.reshape(1, grid, n * n), diag[None], pair[None]
+    return action[None], diag[None], pair[None]
 
 
 def solution(mesh):

time: 48.7 us -> 40.9 us (0.84)
  local copies, waits for them, and re-layouts: 13.7 us -> 8.92 us
  Pallas kernels: 33.7 us -> 30.6 us
    reshape x6 -> x0, local copies, waits for them, and re-layouts: 8.55 us -> none  [the longest x1 2.45 us: per_device(): coup_h3.reshape(-1, n, n)]
    unnamed x17 -> x22, local copies, waits for them, and re-layouts: 5.1 us -> 8.92 us
    pallas_call x1, Pallas kernels: 33.7 us -> 30.6 us  [per_device(): pl.pallas_call(functools.partial(kernel, modes=modes), out_shape=(jax.Sha...]
where the time goes in v2:
time: 40.9 us; the launch traced here: 40.5 us
  Pallas kernels  30.6 us (75%)
  local copies, waits for them, and re-layouts  8.92 us (22%)
  between operations  0.67 us (2%)
    pallas_call x1, Pallas kernels, per_device(): pl.pallas_call(functools.partial(kernel, modes=modes), out_shape=(jax.Sha...  30.6 us
    unnamed x22, local copies, waits for them, and re-layouts  8.92 us

profile of v2, /device:TPU:0, one launch (start us, length us, event | category | flops | bytes accessed | tf_op | source)
XLA Modules:
  0.0 40.5 jit_solution(15200935897049801401)
XLA Ops:
  0.6 0.0 copy-start.7
  0.6 0.7 %copy-done.7 = s32[32,3]{0,1:T(4,128)S(1)} copy-done((s32[32,3]{0,1:T(4,128)S(1)}, s32[32,3]{0,1:T(4,128)}, u32[]{:S(2)}) %copy-start.7) | copy-done | bytes 408
  1.3 0.0 copy-start.5
  1.3 0.1 select_reduce_fusion.1
  1.4 0.1 select_reduce_fusion
  1.6 0.4 %copy-done.5 = f32[1,32,8]{1,2,0:T(8,128)S(1)} copy-done((f32[1,32,8]{1,2,0:T(8,128)S(1)}, f32[1,32,8]{1,2,0:T(8,128)}, u32[]{:S(2)}) %copy-start.5) | copy-done | bytes 1048
  2.0 0.0 copy-start.6
  2.0 0.1 copy.14
  2.1 0.6 %copy-done.6 = f32[32,8]{0,1:T(8,128)S(1)} copy-done((f32[32,8]{0,1:T(8,128)S(1)}, f32[32,8]{0,1:T(8,128)}, u32[]{:S(2)}) %copy-start.6) | copy-done | bytes 1048
  2.7 0.1 copy.15.cv1
  2.8 0.1 copy.16.pairs
  2.9 0.0 copy-start
  2.9 1.0 %copy-done = f32[1,32,4096]{2,1,0:T(8,128)S(1)} copy-done((f32[1,32,4096]{2,1,0:T(8,128)S(1)}, f32[1,32,4096]{2,1,0:T(8,128)}, u32[]{:S(2)}) %copy-start) | copy-done | bytes 524312
  3.9 0.0 copy-start.1
  3.9 1.0 %copy-done.1 = f32[1,32,4096]{2,1,0:T(8,128)S(1)} copy-done((f32[1,32,4096]{2,1,0:T(8,128)S(1)}, f32[1,32,4096]{2,1,0:T(8,128)}, u32[]{:S(2)}) %copy-start.1) | copy-done | bytes 524312
  4.9 0.0 copy-start.2
  4.9 1.0 %copy-done.2 = f32[32,4096]{1,0:T(8,128)S(1)} copy-done((f32[32,4096]{1,0:T(8,128)S(1)}, f32[32,4096]{1,0:T(8,128)}, u32[]{:S(2)}) %copy-start.2) | copy-done | bytes 524312
  6.0 0.0 copy-start.3
  6.0 1.0 %copy-done.3 = f32[32,4096]{1,0:T(8,128)S(1)} copy-done((f32[32,4096]{1,0:T(8,128)S(1)}, f32[32,4096]{1,0:T(8,128)}, u32[]{:S(2)}) %copy-start.3) | copy-done | bytes 524312
  7.0 0.9 %copy-done.4 = f32[1,8,4096]{2,1,0:T(8,128)S(1)} copy-done((f32[1,8,4096]{2,1,0:T(8,128)S(1)}, f32[1,8,4096]{2,1,0:T(8,128)}, u32[]{:S(2)}) %copy-start.4) | copy-done | bytes 131096
  7.9 30.6 %shard_map.103 = (f32[8,4096]{1,0:T(8,128)S(1)}, f32[4,2048]{1,0:T(4,128)S(1)}, f32[4,1984]{1,0:T(4,128)S(1)}) custom-call(f32[8,4096]{1,0:T(8,128)S(1)} %bitcast.11, f32[32,4096]{1,0:T(8,128)S(1)} %bitcast.9, f32[32,4096]{1,0:T(8,128)S(1)} %bitcast.10, f32[32,4096]{1,0:T(8,128)S(1)} %copy-done.2, f32[32,4096]{1,0:T(8,128)S(1)} %copy-done.3, ...), custom_call_target="tpu_custom_call" | custom-call | tf_op jit(solution)/shard_map/pallas_call | solution.py:358
  38.6 0.7 %copy.20 = f32[1,8,4096]{2,1,0:T(8,128)} copy(f32[1,8,4096]{2,1,0:T(8,128)S(1)} %bitcast.12) | data formatting | bytes 262144
  39.2 0.6 %copy.21 = f32[1,4,2048]{2,1,0:T(4,128)} copy(f32[1,4,2048]{2,1,0:T(4,128)S(1)} %bitcast.15) | data formatting | bytes 65536
  39.9 0.6 %copy.22 = f32[1,4,1984]{2,1,0:T(4,128)} copy(f32[1,4,1984]{2,1,0:T(4,128)S(1)} %bitcast.14) | data formatting | bytes 63488
  (4 shorter events, 0.0 us)
Async XLA Ops:
  0.6 0.7 %copy-start.7 = (s32[32,3]{0,1:T(4,128)S(1)}, s32[32,3]{0,1:T(4,128)}, u32[]{:S(2)}) copy-start(s32[32,3]{0,1:T(4,128)} %param.15) | copy-start | bytes 1156
  1.3 0.7 %copy-start.5 = (f32[1,32,8]{1,2,0:T(8,128)S(1)}, f32[1,32,8]{1,2,0:T(8,128)}, u32[]{:S(2)}) copy-start(f32[1,32,8]{1,2,0:T(8,128)} %param.11) | copy-start | bytes 3076
  2.0 0.7 %copy-start.6 = (f32[32,8]{0,1:T(8,128)S(1)}, f32[32,8]{0,1:T(8,128)}, u32[]{:S(2)}) copy-start(f32[32,8]{0,1:T(8,128)} %param.14) | copy-start | bytes 3076
  2.9 1.0 %copy-start = (f32[1,32,4096]{2,1,0:T(8,128)S(1)}, f32[1,32,4096]{2,1,0:T(8,128)}, u32[]{:S(2)}) copy-start(f32[1,32,4096]{2,1,0:T(8,128)} %param.9) | copy-start | bytes 1572868
  3.9 1.0 %copy-start.1 = (f32[1,32,4096]{2,1,0:T(8,128)S(1)}, f32[1,32,4096]{2,1,0:T(8,128)}, u32[]{:S(2)}) copy-start(f32[1,32,4096]{2,1,0:T(8,128)} %param.10) | copy-start | bytes 1572868
  4.9 1.0 %copy-start.2 = (f32[32,4096]{1,0:T(8,128)S(1)}, f32[32,4096]{1,0:T(8,128)}, u32[]{:S(2)}) copy-start(f32[32,4096]{1,0:T(8,128)} %ch2.1) | copy-start | bytes 1572868
  6.0 1.0 %copy-start.3 = (f32[32,4096]{1,0:T(8,128)S(1)}, f32[32,4096]{1,0:T(8,128)}, u32[]{:S(2)}) copy-start(f32[32,4096]{1,0:T(8,128)} %ch3.1) | copy-start | bytes 1572868
  7.0 0.9 %copy-start.4 = (f32[1,8,4096]{2,1,0:T(8,128)S(1)}, f32[1,8,4096]{2,1,0:T(8,128)}, u32[]{:S(2)}) copy-start(f32[1,8,4096]{2,1,0:T(8,128)} %param.8) | copy-start | bytes 393220

commit v3 on v2

--- a/solution.py
+++ b/solution.py
@@ -17,10 +17,6 @@
     return high, (value - high.astype(F32)).astype(BF16)
 
 
-def dot_rows(left, right):
-    return lax.dot_general(left, right, (((1,), (1,)), ((), ())), preferred_element_type=F32)
-
-
 def dot(left, right):
     return jnp.dot(left, right, preferred_element_type=F32)
 
@@ -30,11 +26,11 @@
 
 
 def kernel(
-    a_ref, dh2, dh3, ch2, ch3, dv1, cv1, pairs, slots,
+    a_hbm, dh2_hbm, dh3_hbm, ch2_hbm, ch3_hbm, dv1, cv1, pairs, slots,
     action_ref, diag_ref, pair_ref,
-    gath, d3, c2, c3, acc, a3, aa, hh, hp, xh, xl, yh, yl, psum, arecv, gfield, rows3,
+    a_ref, dh2, dh3, ch2, ch3, gath, d3, c2, c3, acc, a3, aa, hh, hp, xh, xl, yh, yl, psum, arecv, gfield, rows3,
     buf0, buf1, buf2, ra0, ra1, ra2, sb0, sb1, sb2, rb0, rb1, rb2, sc0, sc1, sc2, rc0, rc1, rc2,
-    send, recv, *, modes
+    send, recv, load, *, modes
 ):
     states, grid = gath.shape[0], gath.shape[1]
     n = d3.shape[-1]
@@ -57,9 +53,18 @@
     along = [(st, lax.rem(z + d, ring) * 4 + x * 2 + core) for d in range(1, ring)]
     partners = others + [sibling, across] + along
 
+    loads = [
+        pltpu.make_async_copy(source, target, load.at[i])
+        for i, (source, target) in enumerate(
+            ((a_hbm, a_ref), (dh3_hbm, dh3), (ch3_hbm, ch3), (ch2_hbm, ch2), (dh2_hbm, dh2))
+        )
+    ]
     barrier = pltpu.get_barrier_semaphore()
     for device in partners:
         pl.semaphore_signal(barrier, inc=1, device_id=device, device_id_type=MESH)
+
+    for c in loads:
+        c.start()
 
     numbers = iter(range(10000))
 
@@ -101,13 +106,15 @@
         a3[s, rows, 0:n] = high
         a3[s, rows, n : 2 * n] = low
         a3[s, rows, 2 * n : 3 * n] = high
+        high, low = split(value.T)
         for t in range(2):
-            aa[s, t * n : (t + 1) * n, g * 2 * n + t * n : g * 2 * n + (t + 1) * n] = high
-            aa[s, (2 + t) * n : (3 + t) * n, g * 2 * n + t * n : g * 2 * n + (t + 1) * n] = low
+            rows = pl.ds((2 * g + t) * n, n)
+            aa[s, rows, t * n : (t + 1) * n] = high
+            aa[s, rows, (2 + t) * n : (3 + t) * n] = low
 
     def weights_three(value):
         high, low = split(value)
-        return jnp.concatenate([high, high, low], axis=1)
+        return jnp.concatenate([high, high, low], axis=0)
 
     def store_x(high_ref, low_ref, product, q, weight):
         for k in range(2):
@@ -119,10 +126,9 @@
                 high_ref[rows, g * 2 * n : (g + 1) * 2 * n] = high
                 low_ref[rows, g * 2 * n : (g + 1) * 2 * n] = low
 
-    def field(high_ref, low_ref, s, i):
-        rows = pl.ds(pl.multiple_of(i * 2 * n, 2 * n), 2 * n)
-        both = dot_rows(high_ref[rows, :], aa[s])
-        return both[:, : 2 * n] + both[:, 2 * n :] + dot_rows(low_ref[rows, :], aa[s, 0 : 2 * n])
+    def field(high_ref, low_ref, s, rows):
+        both = dot(high_ref[rows, :], aa[s])
+        return both[:, : 2 * n] + both[:, 2 * n :] + dot(low_ref[rows, :], aa[s, :, 0 : 2 * n])
 
     def store_field(targets, block, i):
         turned = block.T
@@ -135,14 +141,20 @@
 
     def act(left, high_ref, low_ref, gp):
         columns = pl.ds(pl.multiple_of(gp * 4 * n, 4 * n), 4 * n)
+        size = left.shape[0] // 2
         both = dot(left[...], high_ref[:, columns])
-        total = both[: 2 * n] + both[2 * n :] + dot(left[0 : 2 * n], low_ref[:, columns])
+        total = both[:size] + both[size:] + dot(left[0:size], low_ref[:, columns])
         return [
-            total[0:n, k * 2 * n : k * 2 * n + n] + total[n : 2 * n, k * 2 * n + n : (k + 1) * 2 * n]
-            for k in range(2)
+            [
+                total[r : r + n, k * 2 * n : k * 2 * n + n]
+                + total[r + n : r + 2 * n, k * 2 * n + n : (k + 1) * 2 * n]
+                for k in range(2)
+            ]
+            for r in range(0, size, 2 * n)
         ]
 
     aa[...] = jnp.zeros_like(aa)
+    loads[0].wait()
     pl.semaphore_wait(barrier, len(partners))
     coeff_copies = [copy_to(device, a_ref, gath.at[st]) for device in others]
     for c in coeff_copies:
@@ -151,21 +163,28 @@
     tensor = matrices(a_ref[...])
     for g in range(grid):
         load_state(st, g, tensor[g])
+    loads[1].wait()
     spread(dh3, d3)
 
     def diag_group(q):
         value = jnp.concatenate(
             [d3[t * count + 2 * q + k] for k in range(2) for t in range(2)], axis=0
         )
-        product = dot_rows(a3[st], weights_three(value))
+        product = dot(a3[st], weights_three(value.T))
         store_x(xh, xl, product, q, lambda k, t, g: dv1[t * count + 2 * q + k, g])
 
     loop(count // 2, diag_group)
 
+    part = min(count, 8)
+
     def diag_field(i):
-        store_field(((buf0, 0), (buf1, 0)), field(xh, xl, st, i), i)
-
-    loop(count // 2, diag_field)
+        rows = pl.ds(pl.multiple_of(i * part * n, part * n), part * n)
+        total = field(xh, xl, st, rows)
+        for k in range(part // 2):
+            block = total[k * 2 * n : (k + 1) * 2 * n]
+            store_field(((buf0, 0), (buf1, 0)), block, i * (part // 2) + k)
+
+    loop(count // part, diag_field, 1)
 
     def core_start(i):
         c = copy_to(sibling, bufs[i].at[1 - core], ras[i])
@@ -200,7 +219,9 @@
 
     flight = [core_start(0), core_start(1)]
 
+    loads[2].wait()
     spread(ch3, c3)
+    loads[3].wait()
     spread(ch2, c2)
     flight = [x_start(i, flight[i]) for i in range(2)]
 
@@ -218,30 +239,31 @@
     def pair_group(q):
         rows = [row_of(q, k, t) for k in range(2) for t in range(2)]
         value = [c3[pairs[row, 2]] for row in rows]
+        value = jnp.concatenate(value, axis=0).T
         product = None
         for s in range(states):
-            masked = jnp.concatenate(
-                [v * flag(pairs[row, 1] == s) for v, row in zip(value, rows)], axis=0
-            )
-            part = dot_rows(a3[s], weights_three(masked))
+            keep = [flag(pairs[row, 1] == s) for row in rows]
+            keep = jnp.concatenate([lanes(keep[0], keep[1]), lanes(keep[2], keep[3])], axis=1)
+            part = dot(a3[s], weights_three(value * keep))
             product = part if product is None else product + part
         store_x(yh, yl, product, q, lambda k, t, g: cv1[pairs[row_of(q, k, t), 2], g])
 
     loop(pcount // 2, pair_group)
     flight = [z_start(i, flight[i]) for i in range(2)]
 
-    def pair_field(i):
-        total = None
-        for s in range(states):
-            mask = [
-                lanes(*[flag(pairs[row_of(i, k, t), 0] == s) for t in range(2)]) for k in range(2)
-            ]
-            block = field(yh, yl, s, i)
-            block = jnp.concatenate([block[:n] * mask[0], block[n:] * mask[1]], axis=0)
-            total = block if total is None else total + block
-        store_field(((buf2, 0), (buf2, pcount * n)), total, i)
-
-    loop(pcount // 2, pair_field)
+    total = None
+    for s in range(states):
+        block = field(yh, yl, s, slice(None))
+        keep = [
+            lanes(*[flag(pairs[(t * pcount + j) * states + st, 0] == s) for t in range(2)])
+            for j in range(pcount)
+        ]
+        block = jnp.concatenate(
+            [block[j * n : (j + 1) * n] * keep[j] for j in range(pcount)], axis=0
+        )
+        total = block if total is None else total + block
+    for i in range(pcount // 2):
+        store_field(((buf2, 0), (buf2, pcount * n)), total[i * 2 * n : (i + 1) * 2 * n], i)
     pair_flight = core_start(2)
 
     for t in range(2):
@@ -250,29 +272,26 @@
             high, low = split(c2[pairs[row, 2]])
             for s in range(states):
                 keep = flag(pairs[row, 0] == s).astype(BF16)
-                hp[s, t * n : (t + 1) * n, j * n : (j + 1) * n] = high * keep
-                hp[s, (2 + t) * n : (3 + t) * n, j * n : (j + 1) * n] = low * keep
+                top, low_top = (2 * s + t) * n, (2 * states + 2 * s + t) * n
+                hp[top : top + n, j * n : (j + 1) * n] = high * keep
+                hp[low_top : low_top + n, j * n : (j + 1) * n] = low * keep
     pair_flight = x_start(2, pair_flight)
 
-    act_copies = []
-    for d in list(range(1, states)) + [0]:
-        s = lax.rem(st + d, states)
-
-        def pair_act(gp, s=s, d=d):
-            for k, block in enumerate(act(hp.at[s], yh, yl, gp)):
-                if d == 0:
-                    acc[2 * gp + k] = block
-                else:
-                    psum[d - 1, 2 * gp + k] = pack(block)
-
-        loop(grid // 2, pair_act)
-        if d > 0:
-            c = copy_to(others[d - 1], psum.at[d - 1], arecv.at[d - 1])
-            c.start()
-            act_copies.append(c)
-        if d == states - 1:
-            pair_flight = z_start(2, pair_flight)
-
+    def pair_act(gp):
+        for s, blocks in enumerate(act(hp, yh, yl, gp)):
+            for k in range(2):
+                psum[s, 2 * gp + k] = pack(blocks[k])
+
+    loop(grid // 2, pair_act)
+    act_copies = [
+        copy_to(device, psum.at[lax.rem(st + d + 1, states)], arecv.at[d])
+        for d, device in enumerate(others)
+    ]
+    for c in act_copies:
+        c.start()
+    pair_flight = z_start(2, pair_flight)
+
+    loads[4].wait()
     for t in range(0, 2 * count, 8):
         value = matrices(dh2[t : t + 8, :])
         for k in range(8):
@@ -282,10 +301,10 @@
             hh[2 * n + top : 3 * n + top, j * n : (j + 1) * n] = low
 
     def diag_act(gp):
-        for k, block in enumerate(act(hh, xh, xl, gp)):
-            acc[2 * gp + k] = acc[2 * gp + k] + block
-
-    loop(grid // 2, diag_act, 2)
+        for k, block in enumerate(act(hh, xh, xl, gp)[0]):
+            acc[2 * gp + k] = block
+
+    loop(grid // 2, diag_act)
     gfield[st] = finish(2, pair_flight)
     field_copies = [copy_to(device, gfield.at[st], gfield.at[st]) for device in others]
     for c in field_copies:
@@ -295,11 +314,10 @@
     for c in act_copies:
         c.wait()
     for g in range(grid):
-        total = acc[g]
+        packed = psum[st, g]
         for d in range(states - 1):
-            packed = arecv[d, g]
-            total = total + jnp.concatenate([packed[:, :n], packed[:, n:]], axis=0)
-        acc[g] = total
+            packed = packed + arecv[d, g]
+        acc[g] = acc[g] + jnp.concatenate([packed[:, :n], packed[:, n:]], axis=0)
     action_ref[...] = jnp.concatenate(
         [acc[:, pl.ds(0, half, 2), :], acc[:, pl.ds(1, half, 2), :]], axis=-1
     ).reshape(grid, n * n)
@@ -330,21 +348,23 @@
 
     widths = (terms // 2 * n, terms // 2 * n, owned * n)
     vmem = pltpu.VMEM
-    scratch = [
+    scratch = [vmem(coeffs.shape[1:], F32), vmem(diag_h2.shape[1:], F32), vmem(diag_h3.shape[1:], F32)]
+    scratch += [vmem(coup_h2.shape, F32), vmem(coup_h3.shape, F32)]
+    scratch += [
         vmem((states, grid, n * n), F32),
         vmem((terms, n, n), F32),
         vmem(coup_h2.shape[:1] + (n, n), F32),
         vmem(coup_h2.shape[:1] + (n, n), F32),
         vmem((grid, n, n), F32),
         vmem((states, grid * n, 3 * n), BF16),
-        vmem((states, 4 * n, grid * 2 * n), BF16),
+        vmem((states, grid * 2 * n, 4 * n), BF16),
         vmem((4 * n, terms // 2 * n), BF16),
-        vmem((states, 4 * n, owned // 2 * n), BF16),
+        vmem((states * 4 * n, owned // 2 * n), BF16),
         vmem((terms // 2 * n, grid * 2 * n), BF16),
         vmem((terms // 2 * n, grid * 2 * n), BF16),
         vmem((owned // 2 * n, grid * 2 * n), BF16),
         vmem((owned // 2 * n, grid * 2 * n), BF16),
-        vmem((states - 1, grid, n // 2, 2 * n), F32),
+        vmem((states, grid, n // 2, 2 * n), F32),
         vmem((states - 1, grid, n // 2, 2 * n), F32),
         vmem((states, share, owned * n), F32),
         vmem((npairs, share, n), F32),
@@ -353,6 +373,8 @@
         scratch += [vmem(lead + (share, w), F32) for w in widths]
     copies = 3 * (states - 1) + 3 * (ring + 1)
     scratch += [pltpu.SemaphoreType.DMA((copies,)), pltpu.SemaphoreType.DMA((copies,))]
+    scratch += [pltpu.SemaphoreType.DMA((5,))]
+    in_hbm = pl.BlockSpec(memory_space=pltpu.HBM)
     in_vmem = pl.BlockSpec(memory_space=pltpu.VMEM)
     in_smem = pl.BlockSpec(memory_space=pltpu.SMEM)
     action, diag, pair = pl.pallas_call(
@@ -362,7 +384,7 @@
             jax.ShapeDtypeStruct((share, terms * n), F32),
             jax.ShapeDtypeStruct((share, most_slots * n), F32),
         ),
-        in_specs=[in_vmem] * 5 + [in_smem] * 4,
+        in_specs=[in_hbm] * 5 + [in_smem] * 4,
         out_specs=(in_vmem,) * 3,
         scratch_shapes=scratch,
         compiler_params=pltpu.CompilerParams(

time: 40.9 us -> 39.6 us (0.968)
  Pallas kernels: 30.6 us -> 29.3 us
    pallas_call x1, Pallas kernels: 30.6 us -> 29.3 us  [per_device(): pl.pallas_call(functools.partial(kernel, modes=modes), out_shape=(jax.Sha...]
where the time goes in v3:
time: 39.6 us; the launch traced here: 39.2 us
  Pallas kernels  29.3 us (74%)
  local copies, waits for them, and re-layouts  8.92 us (23%)
  between operations  0.67 us (2%)
    pallas_call x1, Pallas kernels, per_device(): pl.pallas_call(functools.partial(kernel, modes=modes), out_shape=(jax.Sha...  29.3 us
    unnamed x22, local copies, waits for them, and re-layouts  8.92 us

profile of v3, /device:TPU:0, one launch (start us, length us, event | category | flops | bytes accessed | tf_op | source)
XLA Modules:
  0.0 39.2 jit_solution(5791758999371658555)
XLA Ops:
  0.6 0.0 copy-start.7
  0.6 0.7 %copy-done.7 = s32[32,3]{0,1:T(4,128)S(1)} copy-done((s32[32,3]{0,1:T(4,128)S(1)}, s32[32,3]{0,1:T(4,128)}, u32[]{:S(2)}) %copy-start.7) | copy-done | bytes 408
  1.3 0.0 copy-start.5
  1.3 0.1 select_reduce_fusion.1
  1.4 0.1 select_reduce_fusion
  1.6 0.4 %copy-done.5 = f32[1,32,8]{1,2,0:T(8,128)S(1)} copy-done((f32[1,32,8]{1,2,0:T(8,128)S(1)}, f32[1,32,8]{1,2,0:T(8,128)}, u32[]{:S(2)}) %copy-start.5) | copy-done | bytes 1048
  2.0 0.0 copy-start.6
  2.0 0.1 copy.14
  2.1 0.6 %copy-done.6 = f32[32,8]{0,1:T(8,128)S(1)} copy-done((f32[32,8]{0,1:T(8,128)S(1)}, f32[32,8]{0,1:T(8,128)}, u32[]{:S(2)}) %copy-start.6) | copy-done | bytes 1048
  2.7 0.1 copy.15.cv1
  2.8 0.1 copy.16.pairs
  2.9 0.0 copy-start
  2.9 1.0 %copy-done = f32[1,32,4096]{2,1,0:T(8,128)S(1)} copy-done((f32[1,32,4096]{2,1,0:T(8,128)S(1)}, f32[1,32,4096]{2,1,0:T(8,128)}, u32[]{:S(2)}) %copy-start) | copy-done | bytes 524312
  3.9 0.0 copy-start.1
  3.9 1.0 %copy-done.1 = f32[1,32,4096]{2,1,0:T(8,128)S(1)} copy-done((f32[1,32,4096]{2,1,0:T(8,128)S(1)}, f32[1,32,4096]{2,1,0:T(8,128)}, u32[]{:S(2)}) %copy-start.1) | copy-done | bytes 524312
  4.9 0.0 copy-start.2
  4.9 1.0 %copy-done.2 = f32[32,4096]{1,0:T(8,128)S(1)} copy-done((f32[32,4096]{1,0:T(8,128)S(1)}, f32[32,4096]{1,0:T(8,128)}, u32[]{:S(2)}) %copy-start.2) | copy-done | bytes 524312
  6.0 0.0 copy-start.3
  6.0 1.0 %copy-done.3 = f32[32,4096]{1,0:T(8,128)S(1)} copy-done((f32[32,4096]{1,0:T(8,128)S(1)}, f32[32,4096]{1,0:T(8,128)}, u32[]{:S(2)}) %copy-start.3) | copy-done | bytes 524312
  7.0 0.9 %copy-done.4 = f32[1,8,4096]{2,1,0:T(8,128)S(1)} copy-done((f32[1,8,4096]{2,1,0:T(8,128)S(1)}, f32[1,8,4096]{2,1,0:T(8,128)}, u32[]{:S(2)}) %copy-start.4) | copy-done | bytes 131096
  7.9 29.3 %shard_map.103 = (f32[8,4096]{1,0:T(8,128)S(1)}, f32[4,2048]{1,0:T(4,128)S(1)}, f32[4,1984]{1,0:T(4,128)S(1)}) custom-call(f32[8,4096]{1,0:T(8,128)S(1)} %bitcast.11, f32[32,4096]{1,0:T(8,128)S(1)} %bitcast.9, f32[32,4096]{1,0:T(8,128)S(1)} %bitcast.10, f32[32,4096]{1,0:T(8,128)S(1)} %copy-done.2, f32[32,4096]{1,0:T(8,128)S(1)} %copy-done.3, ...), custom_call_target="tpu_custom_call" | custom-call | tf_op jit(solution)/shard_map/pallas_call | solution.py:380
  37.3 0.7 %copy.20 = f32[1,8,4096]{2,1,0:T(8,128)} copy(f32[1,8,4096]{2,1,0:T(8,128)S(1)} %bitcast.12) | data formatting | bytes 262144
  37.9 0.6 %copy.21 = f32[1,4,2048]{2,1,0:T(4,128)} copy(f32[1,4,2048]{2,1,0:T(4,128)S(1)} %bitcast.15) | data formatting | bytes 65536
  38.6 0.6 %copy.22 = f32[1,4,1984]{2,1,0:T(4,128)} copy(f32[1,4,1984]{2,1,0:T(4,128)S(1)} %bitcast.14) | data formatting | bytes 63488
  (4 shorter events, 0.0 us)
Async XLA Ops:
  0.6 0.7 %copy-start.7 = (s32[32,3]{0,1:T(4,128)S(1)}, s32[32,3]{0,1:T(4,128)}, u32[]{:S(2)}) copy-start(s32[32,3]{0,1:T(4,128)} %param.15) | copy-start | bytes 1156
  1.3 0.7 %copy-start.5 = (f32[1,32,8]{1,2,0:T(8,128)S(1)}, f32[1,32,8]{1,2,0:T(8,128)}, u32[]{:S(2)}) copy-start(f32[1,32,8]{1,2,0:T(8,128)} %param.11) | copy-start | bytes 3076
  2.0 0.7 %copy-start.6 = (f32[32,8]{0,1:T(8,128)S(1)}, f32[32,8]{0,1:T(8,128)}, u32[]{:S(2)}) copy-start(f32[32,8]{0,1:T(8,128)} %param.14) | copy-start | bytes 3076
  2.9 1.0 %copy-start = (f32[1,32,4096]{2,1,0:T(8,128)S(1)}, f32[1,32,4096]{2,1,0:T(8,128)}, u32[]{:S(2)}) copy-start(f32[1,32,4096]{2,1,0:T(8,128)} %param.9) | copy-start | bytes 1572868
  3.9 1.0 %copy-start.1 = (f32[1,32,4096]{2,1,0:T(8,128)S(1)}, f32[1,32,4096]{2,1,0:T(8,128)}, u32[]{:S(2)}) copy-start(f32[1,32,4096]{2,1,0:T(8,128)} %param.10) | copy-start | bytes 1572868
  4.9 1.0 %copy-start.2 = (f32[32,4096]{1,0:T(8,128)S(1)}, f32[32,4096]{1,0:T(8,128)}, u32[]{:S(2)}) copy-start(f32[32,4096]{1,0:T(8,128)} %ch2_hbm.1) | copy-start | bytes 1572868
  6.0 1.0 %copy-start.3 = (f32[32,4096]{1,0:T(8,128)S(1)}, f32[32,4096]{1,0:T(8,128)}, u32[]{:S(2)}) copy-start(f32[32,4096]{1,0:T(8,128)} %ch3_hbm.1) | copy-start | bytes 1572868
  7.0 0.9 %copy-start.4 = (f32[1,8,4096]{2,1,0:T(8,128)S(1)}, f32[1,8,4096]{2,1,0:T(8,128)}, u32[]{:S(2)}) copy-start(f32[1,8,4096]{2,1,0:T(8,128)} %param.8) | copy-start | bytes 393220

commit v4 on v3

--- a/solution.py
+++ b/solution.py
@@ -388,7 +388,7 @@
         out_specs=(in_vmem,) * 3,
         scratch_shapes=scratch,
         compiler_params=pltpu.CompilerParams(
-            collective_id=0, has_side_effects=True, vmem_limit_bytes=48 * 1024 * 1024
+            collective_id=0, has_side_effects=True, vmem_limit_bytes=61 * 1024 * 1024
         ),
     )(
         coeffs[0],

time: 39.6 us -> 37.6 us (0.949)
  local copies, waits for them, and re-layouts: 8.92 us -> 5.7 us
  Pallas kernels: 29.3 us -> 30.1 us
  other arithmetic: 0.24 us -> 0.78 us
    unnamed x22 -> x16, local copies, waits for them, and re-layouts: 8.92 us -> 5.7 us
    pallas_call x1, Pallas kernels: 29.3 us -> 30.1 us  [per_device(): pl.pallas_call(functools.partial(kernel, modes=modes), out_shape=(jax.Sha...]
    sub x1, other arithmetic: 0.01 us -> 0.55 us  [per_device(): jnp.sum(jnp.where(hit, order[None, :] + 1, 0), axis=1).astype(jnp.int32) - 1]
where the time goes in v4:
time: 37.6 us; the launch traced here: 37.2 us
  Pallas kernels  30.1 us (80%)
  local copies, waits for them, and re-layouts  5.7 us (15%)
  other arithmetic  0.78 us (2%)
  between operations  0.67 us (2%)
    pallas_call x1, Pallas kernels, per_device(): pl.pallas_call(functools.partial(kernel, modes=modes), out_shape=(jax.Sha...  30.1 us
    unnamed x16, local copies, waits for them, and re-layouts  5.7 us

profile of v4, /device:TPU:0, one launch (start us, length us, event | category | flops | bytes accessed | tf_op | source)
XLA Modules:
  0.0 37.2 jit_solution(7869536669675387395)
XLA Ops:
  0.6 0.0 copy-start.4
  0.6 0.7 %copy-done.4 = s32[32,3]{0,1:T(4,128)S(1)} copy-done((s32[32,3]{0,1:T(4,128)S(1)}, s32[32,3]{0,1:T(4,128)}, u32[]{:S(2)}) %copy-start.4) | copy-done | bytes 408
  1.3 0.0 copy-start.2
  1.3 0.1 select_reduce_fusion.1
  1.4 0.1 select_reduce_fusion
  1.6 0.5 %broadcast_add_fusion.slots = s32[31]{0:T(128)} fusion(s32[31]{0:T(128)S(1)} %select_reduce_fusion), kind=kLoop, calls=%fused_computation.8 | loop fusion | flops 31 | bytes 248 | tf_op jit(solution)/shard_map/sub | solution.py:347
  2.1 0.0 copy-done.2
  2.1 0.0 copy-start.3
  2.1 0.7 %copy.14 = f32[1,32,8]{2,1,0:T(8,128)} copy(f32[1,32,8]{1,2,0:T(8,128)S(1)} %copy-done.2) | data formatting | bytes 2048 | tf_op args[3]
  2.8 0.0 copy-done.3
  2.8 0.7 %copy.15.cv1 = f32[32,8]{1,0:T(8,128)} copy(f32[32,8]{0,1:T(8,128)S(1)} %copy-done.3) | data formatting | bytes 2048 | tf_op args[6]
  3.5 0.7 %copy.16.pairs = s32[32,3]{1,0:T(8,128)} copy(s32[32,3]{0,1:T(4,128)S(1)} %copy-done.4) | data formatting | bytes 768 | tf_op args[7]
  4.2 30.1 %shard_map.103 = (f32[8,4096]{1,0:T(8,128)}, f32[4,2048]{1,0:T(4,128)}, f32[4,1984]{1,0:T(4,128)}) custom-call(f32[8,4096]{1,0:T(8,128)} %bitcast.11, f32[32,4096]{1,0:T(8,128)} %bitcast.9, f32[32,4096]{1,0:T(8,128)} %bitcast.10, f32[32,4096]{1,0:T(8,128)} %ch2_hbm.1, f32[32,4096]{1,0:T(8,128)} %ch3_hbm.1, f32[32,8]{1,0:T(8,128)} %bitcast.13, ...), custom_call_target="tpu_custom_call" | custom-call | tf_op jit(solution)/shard_map/pallas_call | solution.py:380
  34.3 0.0 copy-start.1
  34.3 1.6 %copy.20 = f32[1,8,4096]{2,1,0:T(8,128)} copy(f32[1,8,4096]{2,1,0:T(8,128)} %bitcast.12) | data formatting | bytes 262144
  35.9 0.0 copy-done.1
  35.9 0.0 copy-start
  35.9 0.6 %copy.21 = f32[1,4,2048]{2,1,0:T(4,128)} copy(f32[1,4,2048]{2,1,0:T(4,128)S(1)} %bitcast.15) | data formatting | bytes 65536
  36.5 0.2 copy-done
  36.6 0.6 %copy.22 = f32[1,4,1984]{2,1,0:T(4,128)} copy(f32[1,4,1984]{2,1,0:T(4,128)S(1)} %bitcast.14) | data formatting | bytes 63488
  (2 shorter events, 0.0 us)
Async XLA Ops:
  0.6 0.7 %copy-start.4 = (s32[32,3]{0,1:T(4,128)S(1)}, s32[32,3]{0,1:T(4,128)}, u32[]{:S(2)}) copy-start(s32[32,3]{0,1:T(4,128)} %param.15) | copy-start | bytes 1156
  1.3 0.8 %copy-start.2 = (f32[1,32,8]{1,2,0:T(8,128)S(1)}, f32[1,32,8]{1,2,0:T(8,128)}, u32[]{:S(2)}) copy-start(f32[1,32,8]{1,2,0:T(8,128)} %param.11) | copy-start | bytes 3076
  2.1 0.7 %copy-start.3 = (f32[32,8]{0,1:T(8,128)S(1)}, f32[32,8]{0,1:T(8,128)}, u32[]{:S(2)}) copy-start(f32[32,8]{0,1:T(8,128)} %param.14) | copy-start | bytes 3076
  34.3 1.6 %copy-start.1 = (f32[4,2048]{1,0:T(4,128)S(1)}, f32[4,2048]{1,0:T(4,128)}, u32[]{:S(2)}) copy-start(f32[4,2048]{1,0:T(4,128)} %get-tuple-element.7) | copy-start | bytes 98308
  35.9 0.8 %copy-start = (f32[4,1984]{1,0:T(4,128)S(1)}, f32[4,1984]{1,0:T(4,128)}, u32[]{:S(2)}) copy-start(f32[4,1984]{1,0:T(4,128)} %get-tuple-element.8) | copy-start | bytes 95236
